TPU v7x, 256 devices: a whole 4x4x8 slice. The times are simulated.
256 devices in a mesh: slab: 32 (over z, y_lo, core), sub: 8 (over x, y_hi).
Axes of the slice: x: 4, y: 4 (y_hi: 2, y_lo: 2; y = y_hi * 2 + y_lo), z: 8, core: 2. Of those that a mesh axis runs over, the one named last changes fastest.
Arguments:
- positions: float32 [3, 32768], P(None, ('slab', 'sub')), may hold values from 0 to 1
- velocities: float32 [3, 32768], P(None, ('slab', 'sub'))
- species: int32 [32768], P(('slab', 'sub')), may hold values from 0 to 7
- ghost_species: int32 [49152], P(('slab', 'sub')), may hold values from 0 to 7, as said below
- neighbours: int32 [20, 32768], P(None, ('slab', 'sub')), may hold values from 0 to 319, as said below
- slot_mask: int32 [20, 32768], P(None, ('slab', 'sub')), may hold values from 0 to 1, as said below
- edge_vectors: float32 [3, 20, 32768], P(None, None, ('slab', 'sub')), may hold values from -4.8 to 4.8, as said below
- send_slab: int32 [2, 12288], P(None, ('slab', 'sub')), may hold values from 0 to 127, as said below
- send_sub: int32 [2, 12288], P(None, ('slab', 'sub')), may hold values from 0 to 127, as said below
- migrants: int32 [4, 1024], P(None, ('slab', 'sub')), may hold values from 0 to 127, as said below
- embedding: float32 [8, 128], replicated, may hold values from -6 to 6
- energy_shift: float32 [8], replicated, may hold values from -4 to 4
- masses: float32 [8], replicated, may hold values from 0.5 to 4
- radial_one_in: float32 [64, 8], replicated, may hold values from -2 to 2
- radial_one_mid: float32 [2, 64, 64], replicated, may hold values from -0.75 to 0.75
- radial_one_out: float32 [256, 64], replicated, may hold values from -0.75 to 0.75
- node_one: float32 [6, 128, 128], replicated, may hold values from -0.5 to 0.5
- radial_two_in: float32 [64, 8], replicated, may hold values from -2 to 2
- radial_two_mid: float32 [2, 64, 64], replicated, may hold values from -0.75 to 0.75
- radial_two_out: float32 [512, 64], replicated, may hold values from -0.75 to 0.75
- node_two: float32 [5, 128, 128], replicated, may hold values from -0.5 to 0.5
- readout_linear: float32 [128], replicated, may hold values from -0.5 to 0.5
- readout_hidden: float32 [16, 128], replicated, may hold values from -0.5 to 0.5
- readout_out: float32 [16], replicated, may hold values from -1.5 to 1.5
- box_matrix: float32 [3, 3], replicated, as said below
- box_velocity: float32 [3, 3], replicated, may hold values from -3 to 3
Outputs:
- atom_energy: float32 [32768], P(('slab', 'sub'))
- forces: float32 [3, 32768], P(None, ('slab', 'sub'))
- new_velocities: float32 [3, 32768], P(None, ('slab', 'sub'))
- new_positions: float32 [3, 32768], P(None, ('slab', 'sub'))
- arrivals: float32 [6, 4096], P(None, ('slab', 'sub'))
- new_box: float32 [3, 3], replicated
- new_box_velocity: float32 [3, 3], replicated
Inputs may be any that keep to these rules, and one draw needn't show every extreme that they name: `neighbours`: the 20 entries of an atom are distinct extended rows of its device. `slot_mask`: live slots of an atom come first; every atom has 10 to 20 live slots and the first atom of each device has all 20. `edge_vectors`: every edge vector has a length between 1.8 and 4.8. `send_slab`: each row holds, for each device, 48 distinct own atoms; row 0 goes to slab index - 1, row 1 to slab index + 1. `send_sub`: each row holds, for each device, 48 distinct own atoms; row 0 goes to sub index - 1, row 1 to sub index + 1. `migrants`: for each device the four rows hold 16 distinct own atoms, moving to slab index - 1, slab index + 1, sub index - 1 and sub index + 1. `ghost_species`: each ghost row holds the species of the atom that the send lists deliver to it. `box_matrix`: the diagonal dominates each row, so the determinant is positive.
All inputs are finite; a program needn't handle non-finite values.
Results may differ from a plain program's by a relative error of at most 0.000061.
Values sent between devices are 32-bit elements; how exact they have to be, the bound alone decides.
A program may use at most 128 MiB of HBM per device.

v0:
```python
import functools

import jax
import jax.numpy as jnp
from jax import lax
from jax.experimental import pallas as pl
from jax.experimental.pallas import tpu as pltpu
from jax.sharding import PartitionSpec as P

MESH = pl.DeviceIdType.MESH
F32 = jnp.float32
BF16 = jnp.bfloat16
HIGHEST = lax.Precision.HIGHEST

cutoff = 5.0
neighbor_norm = 0.125
time_step = 0.5
outside_pressure = 0.5
box_mass = 0.125

C = 128
A = 128
K = 20
GH = 48
EXT = A + 4 * GH
CH = 4
NCH = K // CH
W = CH * A
E = K * A
RH = 64
LO = 2


def split2(x):
    high = x.astype(BF16)
    return high, (x - high.astype(F32)).astype(BF16)


def split3(x):
    high = x.astype(BF16).astype(F32)
    rest = x - high
    middle = rest.astype(BF16).astype(F32)
    return high, middle, rest - middle


def stack_left(weights):
    high, low = split2(weights)
    return jnp.concatenate([high, high, low], axis=1)


def stack_right(values):
    high, low = split2(values)
    return jnp.concatenate([high, low, high], axis=0)


def mm(left, right):
    return jnp.dot(left, right, preferred_element_type=F32)


def mm_nt(left, right):
    return lax.dot_general(left, right, (((1,), (1,)), ((), ())), preferred_element_type=F32)


def mix(weights, values):
    return mm(stack_left(weights), stack_right(values))


def logistic(x):
    return 1.0 / (1.0 + jnp.exp(-x))


def radial_net(start, win, mid0, mid1, out):
    pre = mm(win, start)
    for after in (mid0, mid1, out):
        half = pre.shape[1] // 2
        value, slope = pre[:, :half], pre[:, half:]
        gate = logistic(value)
        active = value * gate
        moved = (gate + active * (1.0 - gate)) * slope
        pre = mm(after, stack_right(jnp.concatenate([active, moved], axis=1)))
    return pre


def kernel(slabs, subs, *refs):
    (
        positions, velocities, species, ghost_species, neighbours, slot_mask, edges, send_slab, send_sub, migrants,
        embedding, energy_shift, masses, one_in, one_mid, one_out, node_one, two_in, two_mid, two_out, node_two,
        readout_linear, readout_hidden, readout_out, box_matrix, box_velocity,
        energy_out, forces_out, velocities_out, positions_out, arrivals_out, box_out, box_velocity_out,
        lists, geo, basis, hot, kept1, radial1, radial2, sums, pairs, table, parts, gather_parts,
        packed, gflat, send_a, recv_a, scat, recv_b, push, recv_c, send_d, recv_d, stage1, stage2,
        part1, part2, send_sem, recv_sem, sum_send, sum_recv,
    ) = refs
    slab, sub = lax.axis_index("slab"), lax.axis_index("sub")
    low, high = lax.rem(slab, LO), slab // LO
    many1, many2 = LO * subs, slabs // LO
    mine1 = low * subs + sub

    def first_peer(step):
        flat = lax.rem(mine1 + step, many1)
        return (high * LO + flat // subs, lax.rem(flat, subs))

    def second_peer(step):
        return (lax.rem(high + step, many2) * LO + low, sub)

    around = (
        (lax.rem(slab + slabs - 1, slabs), sub),
        (lax.rem(slab + 1, slabs), sub),
        (slab, lax.rem(sub + subs - 1, subs)),
        (slab, lax.rem(sub + 1, subs)),
    )
    barrier = pltpu.get_barrier_semaphore()

    def greet(device):
        pl.semaphore_signal(barrier, inc=1, device_id=device, device_id_type=MESH)

    for device in around:
        greet(device)

    @pl.loop(1, many1)
    def _(step):
        greet(first_peer(step))

    @pl.loop(1, many2)
    def _(step):
        greet(second_peer(step))

    def exchange(number, source, target):
        copies = []
        for block in range(4):
            copy = pltpu.make_async_remote_copy(
                src_ref=source(block),
                dst_ref=target(block ^ 1),
                send_sem=send_sem.at[number, block],
                recv_sem=recv_sem.at[number, block ^ 1],
                device_id=around[block],
                device_id_type=MESH,
            )
            copy.start()
            copies.append(copy)
        return copies

    def rows(block):
        return pl.ds(block * GH, GH)

    lane = lax.broadcasted_iota(jnp.int32, (1, A), 1)

    lists[...] = jnp.zeros_like(lists)
    lists[0:2, 0:GH] = send_slab[...].astype(F32)
    lists[2:4, 0:GH] = send_sub[...].astype(F32)
    columns = lists[...].T
    lanes_f = lax.broadcasted_iota(jnp.int32, (GH, A), 1).astype(F32)
    sent_f = jnp.concatenate(
        [(lanes_f == columns[0:GH, q : q + 1]).astype(F32) for q in range(4)], axis=0
    )
    sent_rows = sent_f.astype(BF16)
    sent_columns = sent_f.T.astype(BF16)

    ex, ey, ez = edges[0], edges[1], edges[2]
    distance = jnp.sqrt(ex * ex + ey * ey + ez * ez)
    inverse_distance = 1.0 / distance
    unit = (ex / distance, ey / distance, ez / distance)
    weight = slot_mask[...].astype(F32) * neighbor_norm
    for row, values in enumerate(unit + (weight, distance, inverse_distance)):
        for k in range(K):
            geo[row : row + 1, k * A : (k + 1) * A] = values[k : k + 1, :]

    kinds = lax.broadcasted_iota(jnp.int32, (8, A), 0)
    own_kind = (kinds == species[...]).astype(F32)
    ghost_kinds = lax.broadcasted_iota(jnp.int32, (8, 4 * GH), 0)
    ghost_kind = (ghost_kinds == ghost_species[...]).astype(F32)
    pad8 = jnp.zeros((8, A), F32)
    own_kind16 = jnp.concatenate([own_kind, pad8], axis=0).astype(BF16)
    ghost_kind16 = jnp.concatenate([ghost_kind, jnp.zeros((8, 4 * GH), F32)], axis=0).astype(BF16)

    orders = (lax.broadcasted_iota(jnp.int32, (8, 1), 0) + 1).astype(F32) * jnp.pi
    scale = jnp.sqrt(2.0 / cutoff).astype(F32)

    one_in_s = jnp.concatenate(
        [part for part in (lambda h, m, l: (h, h, h, m, m, l))(*split3(one_in[...].T))], axis=0
    ).T.astype(BF16)
    two_in_s = jnp.concatenate(
        [part for part in (lambda h, m, l: (h, h, h, m, m, l))(*split3(two_in[...].T))], axis=0
    ).T.astype(BF16)
    one_mid0, one_mid1 = stack_left(one_mid[0]), stack_left(one_mid[1])
    one_out_s = stack_left(one_out[...])

    lifted = lax.dot_general(
        embedding[...], node_one[0], (((1,), (1,)), ((), ())), precision=HIGHEST, preferred_element_type=F32
    )
    lifted_s = jnp.concatenate(list(split3(lifted)) + [pad8], axis=0).T.astype(BF16)

    sums[...] = jnp.zeros_like(sums)

    def lanes_of(chunk):
        return pl.ds(pl.multiple_of(chunk * W, W), W)

    def first_forward(chunk, _):
        here = lanes_of(chunk)
        row_of = lax.broadcasted_iota(jnp.int32, (EXT, A), 0)
        for j in range(CH):
            picked = neighbours[pl.ds(chunk * CH + j, 1), :]
            hot[chunk, :, j * A : (j + 1) * A] = (row_of == picked).astype(F32).astype(BF16)
        d = geo[4:5, here]
        inverse_d = geo[5:6, here]
        x = d / cutoff
        x2 = x * x
        x3 = x2 * x
        x5 = x2 * x3
        x6 = x3 * x3
        envelope = 1.0 - 28.0 * x6 + 48.0 * x6 * x - 21.0 * x6 * x2
        slope = (-168.0 * x5 + 336.0 * x6 - 168.0 * x6 * x) / cutoff
        angle = orders * x
        sine, cosine = jnp.sin(angle), jnp.cos(angle)
        even = scale * inverse_d * envelope
        values = sine * even
        slopes = cosine * (orders / cutoff) * even + sine * (scale * inverse_d * (slope - envelope * inverse_d))
        h, m, l = split3(jnp.concatenate([values, slopes], axis=1))
        start = jnp.concatenate([h, m, l, h, m, h], axis=0).astype(BF16)
        basis[chunk] = start
        radial1[...] = radial_net(start, one_in_s, one_mid0, one_mid1, one_out_s)
        kind = mm(own_kind16, hot[chunk, 0:A, :]) + mm(ghost_kind16, hot[chunk, A:EXT, :])
        kind8 = kind[0:8]
        picked_x = mm(lifted_s, jnp.concatenate([kind8, kind8, kind8, jnp.zeros_like(kind8)], axis=0).astype(BF16))
        total = [jnp.zeros((C, A), F32) for _ in range(4)]
        for j in range(CH):
            cut = slice(j * A, (j + 1) * A)
            far = slice(W + j * A, W + (j + 1) * A)
            at = pl.ds(pl.multiple_of(chunk * W + j * A, A), A)
            wx = picked_x[:, cut] * geo[3:4, at]
            total[0] += radial1[0:C, cut] * wx
            q1 = radial1[C : 2 * C, cut] * wx
            for a in range(3):
                total[a + 1] += geo[a : a + 1, at] * q1
            kept1[chunk, 0:C, cut] = q1
            kept1[chunk, C : 2 * C, cut] = radial1[0:C, far] * wx
            kept1[chunk, 2 * C : 3 * C, cut] = radial1[C : 2 * C, far] * wx
        for a in range(4):
            sums[a] += total[a]
        return 0

    lax.fori_loop(0, NCH, first_forward, 0)

    s0 = mm(
        jnp.concatenate(list(split3(embedding[...])) + [pad8], axis=0).T.astype(BF16),
        jnp.concatenate([own_kind, own_kind, own_kind, pad8], axis=0).astype(BF16),
    )
    a0 = sums[0]
    a1 = [sums[1], sums[2], sums[3]]
    square = a1[0] * a1[0] + a1[1] * a1[1] + a1[2] * a1[2]
    s1 = s0 + mix(node_one[1], a0) + mix(node_one[2], a0 * a0) + mix(node_one[3], square)
    turned = mix(node_one[4], jnp.concatenate(a1, axis=1))
    gate1 = mix(node_one[5], a0)
    v1 = jnp.concatenate([turned[:, a * A : (a + 1) * A] + gate1 * a1[a] for a in range(3)], axis=1)
    lifted_x = mix(node_two[0], s1)
    lifted_y = mix(node_two[1], v1)
    own_table = jnp.concatenate([lifted_x] + [lifted_y[:, a * A : (a + 1) * A] for a in range(3)], axis=0)
    own_high, own_low = split2(own_table)
    send_a[...] = mm_nt(sent_rows, own_high) + mm_nt(sent_rows, own_low)
    table[:, 0:A] = own_high
    table[:, A : 2 * A] = own_low

    pl.semaphore_wait(barrier, 4 + many1 - 1 + many2 - 1)
    copies_a = exchange(0, lambda q: send_a.at[rows(q)], lambda q: recv_a.at[rows(q)])

    two_mid0, two_mid1 = stack_left(two_mid[0]), stack_left(two_mid[1])
    two_out_s = stack_left(two_out[...])

    def second_radial(chunk, _):
        radial2[chunk] = radial_net(basis[chunk], two_in_s, two_mid0, two_mid1, two_out_s)
        return 0

    lax.fori_loop(0, NCH, second_radial, 0)

    for copy in copies_a:
        copy.wait_recv()
    ghost_high, ghost_low = split2(recv_a[...].T)
    gather_parts[:, 0 : 4 * GH] = ghost_high
    gather_parts[:, 4 * GH : 8 * GH] = ghost_low

    sums2 = parts
    sums2[...] = jnp.zeros_like(sums2)

    def second_forward(chunk, _):
        own_hot = hot[chunk, 0:A, :]
        far_hot = hot[chunk, A:EXT, :]
        pairs[chunk] = mm(table[...], jnp.concatenate([own_hot, own_hot], axis=0)) + mm(
            gather_parts[...], jnp.concatenate([far_hot, far_hot], axis=0)
        )
        total = [jnp.zeros((C, A), F32) for _ in range(4)]
        for j in range(CH):
            cut = slice(j * A, (j + 1) * A)
            at = pl.ds(pl.multiple_of(chunk * W + j * A, A), A)
            w = geo[3:4, at]
            u = [geo[a : a + 1, at] for a in range(3)]
            wx = pairs[chunk, 0:C, cut] * w
            wy = [pairs[chunk, (a + 1) * C : (a + 2) * C, cut] * w for a in range(3)]
            along = wy[0] * u[0] + wy[1] * u[1] + wy[2] * u[2]
            total[0] += radial2[chunk, 0:C, cut] * wx + radial2[chunk, 3 * C : 4 * C, cut] * along
            r1x = radial2[chunk, C : 2 * C, cut] * wx
            r2 = radial2[chunk, 2 * C : 3 * C, cut]
            for a in range(3):
                total[a + 1] += r1x * u[a] + r2 * wy[a]
        for a in range(4):
            sums2[a] += total[a]
        return 0

    lax.fori_loop(0, NCH, second_forward, 0)

    b0 = sums2[0]
    b1 = [sums2[1], sums2[2], sums2[3]]
    square2 = b1[0] * b1[0] + b1[1] * b1[1] + b1[2] * b1[2]
    s2 = s1 + mix(node_two[2], b0) + mix(node_two[3], b0 * b0) + mix(node_two[4], square2)
    pre = mix(readout_hidden[...], s2)
    gate2 = logistic(pre)
    hidden = pre * gate2
    linear = jnp.broadcast_to(readout_linear[...], (A, C)).T
    outer = jnp.broadcast_to(readout_out[...], (A, 16)).T
    shift = jnp.zeros((1, A), F32)
    mass = jnp.zeros((1, A), F32)
    for s in range(8):
        shift = jnp.where(species[...] == s, energy_shift[s], shift)
        mass = jnp.where(species[...] == s, masses[s], mass)
    energy_out[...] = (
        shift + jnp.sum(linear * s1, axis=0, keepdims=True) + jnp.sum(outer * hidden, axis=0, keepdims=True)
    )
    back_pre = outer * (gate2 + hidden * (1.0 - gate2))
    back_s2 = mix(readout_hidden[...].T, back_pre)
    back_b0 = mix(node_two[2].T, back_s2) + 2.0 * b0 * mix(node_two[3].T, back_s2)
    back_square2 = 2.0 * mix(node_two[4].T, back_s2)
    sums2[0] = back_b0
    for a in range(3):
        sums2[a + 1] = b1[a] * back_square2

    scat[...] = jnp.zeros_like(scat)

    def second_back(chunk, _):
        for j in range(CH):
            cut = slice(j * A, (j + 1) * A)
            far = slice(W + j * A, W + (j + 1) * A)
            at = pl.ds(pl.multiple_of(chunk * W + j * A, A), A)
            w = geo[3:4, at]
            u = [geo[a : a + 1, at] for a in range(3)]
            wb0 = sums2[0] * w
            wb1 = [sums2[a + 1] * w for a in range(3)]
            dot_u = wb1[0] * u[0] + wb1[1] * u[1] + wb1[2] * u[2]
            back = [radial2[chunk, 0:C, cut] * wb0 + radial2[chunk, C : 2 * C, cut] * dot_u]
            r3b0 = radial2[chunk, 3 * C : 4 * C, cut] * wb0
            r2 = radial2[chunk, 2 * C : 3 * C, cut]
            for a in range(3):
                back.append(r3b0 * u[a] + r2 * wb1[a])
            for a in range(4):
                h, l = split2(back[a])
                kept = slice(a * C, (a + 1) * C)
                packed[kept, cut] = h
                packed[kept, far] = l
        hot_here = hot[chunk]
        scat[...] += mm_nt(hot_here, packed[:, 0:W]) + mm_nt(hot_here, packed[:, W : 2 * W])
        return 0

    lax.fori_loop(0, NCH, second_back, 0)
    copies_b = exchange(1, lambda q: scat.at[pl.ds(A + q * GH, GH)], lambda q: recv_b.at[rows(q)])

    def second_edges(chunk, _):
        for j in range(CH):
            cut = slice(j * A, (j + 1) * A)
            far = slice(W + j * A, W + (j + 1) * A)
            at = pl.ds(pl.multiple_of(chunk * W + j * A, A), A)
            w = geo[3:4, at]
            u = [geo[a : a + 1, at] for a in range(3)]
            k0 = sums2[0]
            k1 = [sums2[a + 1] for a in range(3)]
            x = pairs[chunk, 0:C, cut]
            y = [pairs[chunk, (a + 1) * C : (a + 2) * C, cut] for a in range(3)]
            dot_u = k1[0] * u[0] + k1[1] * u[1] + k1[2] * u[2]
            along = y[0] * u[0] + y[1] * u[1] + y[2] * u[2]
            cross = y[0] * k1[0] + y[1] * k1[1] + y[2] * k1[2]
            stretch = (
                (radial2[chunk, 0:C, far] * k0 + radial2[chunk, C : 2 * C, far] * dot_u) * x
                + radial2[chunk, 3 * C : 4 * C, far] * along * k0
                + radial2[chunk, 2 * C : 3 * C, far] * cross
            )
            gflat[3:4, at] = w * jnp.sum(stretch, axis=0, keepdims=True)
            r3k0 = radial2[chunk, 3 * C : 4 * C, cut] * k0
            r1x = radial2[chunk, C : 2 * C, cut] * x
            for a in range(3):
                gflat[a : a + 1, at] = w * jnp.sum(r3k0 * y[a] + r1x * k1[a], axis=0, keepdims=True)
        return 0

    lax.fori_loop(0, NCH, second_edges, 0)

    for copy in copies_b:
        copy.wait_recv()
    back_high, back_low = split2(recv_b[...])
    back_table = (scat[0:A] + mm(sent_columns, back_high) + mm(sent_columns, back_low)).T
    back_s1 = back_s2 + linear + mix(node_two[0].T, back_table[0:C])
    back_v1 = mix(
        node_two[1].T, jnp.concatenate([back_table[(a + 1) * C : (a + 2) * C] for a in range(3)], axis=1)
    )
    back_turned = mix(node_one[4].T, back_v1)
    back_square = 2.0 * mix(node_one[3].T, back_s1)
    cut_v = [back_v1[:, a * A : (a + 1) * A] for a in range(3)]
    back_gate = a1[0] * cut_v[0] + a1[1] * cut_v[1] + a1[2] * cut_v[2]
    sums[0] = (
        mix(node_one[1].T, back_s1) + 2.0 * a0 * mix(node_one[2].T, back_s1) + mix(node_one[5].T, back_gate)
    )
    for a in range(3):
        sums[a + 1] = back_turned[:, a * A : (a + 1) * A] + gate1 * cut_v[a] + a1[a] * back_square

    push[...] = jnp.zeros_like(push)

    def first_edges(chunk, _):
        pieces = []
        for j in range(CH):
            cut = slice(j * A, (j + 1) * A)
            at = pl.ds(pl.multiple_of(chunk * W + j * A, A), A)
            u = [geo[a : a + 1, at] for a in range(3)]
            inverse_d = geo[5:6, at]
            k1 = [sums[a + 1] for a in range(3)]
            q1 = kept1[chunk, 0:C, cut]
            dot_u = k1[0] * u[0] + k1[1] * u[1] + k1[2] * u[2]
            stretch = gflat[3:4, at] + jnp.sum(
                kept1[chunk, C : 2 * C, cut] * sums[0] + kept1[chunk, 2 * C : 3 * C, cut] * dot_u,
                axis=0,
                keepdims=True,
            )
            turn = [gflat[a : a + 1, at] + jnp.sum(q1 * k1[a], axis=0, keepdims=True) for a in range(3)]
            inward = turn[0] * u[0] + turn[1] * u[1] + turn[2] * u[2]
            radial_part = stretch - inward * inverse_d
            for a in range(3):
                gflat[a : a + 1, at] = radial_part * u[a] + turn[a] * inverse_d
            gflat[3:8, at] = jnp.zeros((5, A), F32)
        g = gflat[:, lanes_of(chunk)]
        g_high = g.astype(BF16).astype(F32)
        both = jnp.concatenate([g_high, g - g_high], axis=0).astype(BF16)
        push[...] += mm_nt(hot[chunk], both)
        return 0

    lax.fori_loop(0, NCH, first_edges, 0)
    pushed = push[...]
    pushed = pushed[:, 0:8] + pushed[:, 8:16]
    push[:, 0:8] = pushed
    copies_c = exchange(2, lambda q: push.at[pl.ds(A + q * GH, GH)], lambda q: recv_c.at[rows(q)])

    own = jnp.zeros((8, A), F32)
    virial = [[jnp.zeros((1, A), F32) for _ in range(3)] for _ in range(3)]
    for k in range(K):
        own += gflat[:, k * A : (k + 1) * A]
        for a in range(3):
            for b in range(3):
                virial[a][b] += edges[a, k : k + 1, :] * gflat[b : b + 1, k * A : (k + 1) * A]
    for copy in copies_c:
        copy.wait_recv()
    come_high, come_low = split2(recv_c[...])
    back_f = (push[0:A] + mm(sent_columns, come_high) + mm(sent_columns, come_low)).T
    forces = own[0:3] - back_f[0:3]
    forces_out[...] = forces
    new_velocities = velocities[...] + time_step * forces / mass
    velocities_out[...] = new_velocities

    order = (1, 0, 3, 2)
    movers = jnp.full((1, A), -1, jnp.int32)
    for q in range(4):
        for j in range(4):
            movers = jnp.where(lane == 4 * q + j, migrants[order[q], j], movers)
    chosen = (lax.broadcasted_iota(jnp.int32, (A, A), 0) == movers).astype(F32).astype(BF16)
    state = jnp.concatenate([positions[...], new_velocities, jnp.zeros((2, A), F32)], axis=0)
    h, m, l = split3(state)
    sent_state = mm(jnp.concatenate([h, m, l, jnp.zeros_like(h)], axis=0).astype(BF16), chosen)
    send_d[...] = sent_state[0:8] + sent_state[8:16] + sent_state[16:24]
    copies_d = exchange(3, lambda q: send_d, lambda q: recv_d.at[q])

    mine = jnp.zeros((1, A), F32)
    for a in range(3):
        for b in range(3):
            term = new_velocities[a : a + 1] * mass * new_velocities[b : b + 1] - virial[a][b]
            mine = jnp.where(lane == 3 * a + b, jnp.sum(term, axis=1, keepdims=True), mine)

    def all_sum(number, value, part, stage, many, me, peer):
        part[...] = value.reshape(1, 1, A)
        stage[pl.ds(me, 1)] = value.reshape(1, 1, A)

        @pl.loop(1, many)
        def _(step):
            pltpu.make_async_remote_copy(
                src_ref=part,
                dst_ref=stage.at[pl.ds(me, 1)],
                send_sem=sum_send.at[number],
                recv_sem=sum_recv.at[number],
                device_id=peer(step),
                device_id_type=MESH,
            ).start()

        whole = stage.at[pl.ds(0, many - 1)]
        pltpu.make_async_copy(whole, whole, sum_recv.at[number]).wait()
        pltpu.make_async_copy(whole, whole, sum_send.at[number]).wait()
        return jnp.sum(stage[...], axis=0)

    near = all_sum(0, mine, part1, stage1, many1, mine1, first_peer)
    stress_row = all_sum(1, near, part2, stage2, many2, high, second_peer)

    def entry(ref, a, b):
        return jnp.full((1, A), ref[a, b], F32)

    def determinant(m):
        return (
            m[0][0] * (m[1][1] * m[2][2] - m[1][2] * m[2][1])
            - m[0][1] * (m[1][0] * m[2][2] - m[1][2] * m[2][0])
            + m[0][2] * (m[1][0] * m[2][1] - m[1][1] * m[2][0])
        )

    def inverse(m):
        det = determinant(m)
        cof = [
            [
                m[(r + 1) % 3][(c + 1) % 3] * m[(r + 2) % 3][(c + 2) % 3]
                - m[(r + 1) % 3][(c + 2) % 3] * m[(r + 2) % 3][(c + 1) % 3]
                for c in range(3)
            ]
            for r in range(3)
        ]
        return [[cof[c][r] / det for c in range(3)] for r in range(3)]

    box = [[entry(box_matrix, a, b) for b in range(3)] for a in range(3)]
    volume = determinant(box)
    inv = inverse(box)
    total_atoms = box_mass * (A * slabs * subs)
    pressed = []
    for a in range(3):
        line = []
        for b in range(3):
            value = jnp.broadcast_to(stress_row[:, 3 * a + b : 3 * a + b + 1], (1, A))
            line.append(value - outside_pressure * volume if a == b else value)
        pressed.append(line)
    box_speed = []
    for a in range(3):
        line = []
        for b in range(3):
            pushed_box = pressed[a][0] * inv[b][0] + pressed[a][1] * inv[b][1] + pressed[a][2] * inv[b][2]
            line.append(entry(box_velocity, a, b) + time_step * pushed_box / total_atoms)
        box_speed.append(line)
    new_box = [[box[a][b] + time_step * box_speed[a][b] for b in range(3)] for a in range(3)]
    new_inverse = inverse(new_box)
    for a in range(3):
        for b in range(3):
            box_out[a : a + 1, b : b + 1] = new_box[a][b][:, 0:1]
            box_velocity_out[a : a + 1, b : b + 1] = box_speed[a][b][:, 0:1]

    def drift(moving):
        return [
            new_inverse[a][0] * moving[0:1] + new_inverse[a][1] * moving[1:2] + new_inverse[a][2] * moving[2:3]
            for a in range(3)
        ]

    moved = drift(new_velocities)
    for a in range(3):
        positions_out[a : a + 1, :] = positions[a : a + 1, :] + time_step * moved[a]
    for copy in copies_d:
        copy.wait_recv()
    come = jnp.where(
        lane < 4, recv_d[0], jnp.where(lane < 8, recv_d[1], jnp.where(lane < 12, recv_d[2], recv_d[3]))
    )
    moved = drift(come[3:6])
    for a in range(3):
        arrivals_out[a : a + 1, :] = (come[a : a + 1] + time_step * moved[a])[:, 0:16]
    arrivals_out[3:6, :] = come[3:6, 0:16]

    for copies in (copies_a, copies_b, copies_c, copies_d):
        for copy in copies:
            copy.wait_send()


def solution(mesh):
    slabs, subs = mesh.shape["slab"], mesh.shape["sub"]
    many1, many2 = LO * subs, slabs // LO
    vmem = pl.BlockSpec(memory_space=pltpu.VMEM)
    smem = pl.BlockSpec(memory_space=pltpu.SMEM)
    in_smem = {9, 11, 12, 24, 25}

    def body(*arrays):
        arrays = list(arrays)
        for position in (2, 3, 21, 23):
            arrays[position] = arrays[position].reshape(1, -1)
        shapes = [(1, A), (3, A), (3, A), (3, A), (6, 16), (3, 3), (3, 3)]
        outs = pl.pallas_call(
            functools.partial(kernel, slabs, subs),
            out_shape=[jax.ShapeDtypeStruct(shape, F32) for shape in shapes],
            in_specs=[smem if i in in_smem else vmem for i in range(26)],
            out_specs=[vmem] * 7,
            scratch_shapes=[
                pltpu.VMEM((8, 128), F32),
                pltpu.VMEM((8, E), F32),
                pltpu.VMEM((NCH, 48, 2 * W), BF16),
                pltpu.VMEM((NCH, EXT, W), BF16),
                pltpu.VMEM((NCH, 3 * C, W), F32),
                pltpu.VMEM((2 * C, 2 * W), F32),
                pltpu.VMEM((NCH, 4 * C, 2 * W), F32),
                pltpu.VMEM((4, C, A), F32),
                pltpu.VMEM((NCH, 4 * C, W), F32),
                pltpu.VMEM((4 * C, 2 * A), BF16),
                pltpu.VMEM((4, C, A), F32),
                pltpu.VMEM((4 * C, 8 * GH), BF16),
                pltpu.VMEM((4 * C, 2 * W), BF16),
                pltpu.VMEM((8, E), F32),
                pltpu.VMEM((4 * GH, 4 * C), F32),
                pltpu.VMEM((4 * GH, 4 * C), F32),
                pltpu.VMEM((EXT, 4 * C), F32),
                pltpu.VMEM((4 * GH, 4 * C), F32),
                pltpu.VMEM((EXT, 16), F32),
                pltpu.VMEM((4 * GH, 16), F32),
                pltpu.VMEM((8, A), F32),
                pltpu.VMEM((4, 8, A), F32),
                pltpu.VMEM((many1, 1, A), F32),
                pltpu.VMEM((many2, 1, A), F32),
                pltpu.VMEM((1, 1, A), F32),
                pltpu.VMEM((1, 1, A), F32),
                pltpu.SemaphoreType.DMA((4, 4)),
                pltpu.SemaphoreType.DMA((4, 4)),
                pltpu.SemaphoreType.DMA((2,)),
                pltpu.SemaphoreType.DMA((2,)),
            ],
            compiler_params=pltpu.CompilerParams(
                collective_id=0, has_side_effects=True, vmem_limit_bytes=56 * 1024 * 1024
            ),
            name="step",
        )(*arrays)
        return (outs[0].reshape(A),) + tuple(outs[1:])

    tail = P(None, ("slab", "sub"))
    flat = P(("slab", "sub"))
    placed = (tail, tail, flat, flat, tail, tail, P(None, None, ("slab", "sub")), tail, tail, tail) + (P(),) * 16
    return jax.shard_map(
        body,
        mesh=mesh,
        in_specs=placed,
        out_specs=(flat, tail, tail, tail, tail, P(), P()),
        check_vma=False,
    )
```

profile of v0, /device:TPU:8, one launch (start us, length us, event | category | flops | bytes accessed | tf_op | source)
XLA Modules:
  0.0 69.2 jit_solution(3140114773975120986)
XLA Ops:
  0.6 0.0 copy-start.1
  0.6 0.0 copy-start
  0.7 1.4 %copy.33.refs_13_ = f32[64,8]{1,0:T(8,128)} copy(f32[64,8]{0,1:T(8,128)} %param.39) | data formatting | bytes 4096 | tf_op args[13]
  2.1 1.4 %copy.35.refs_17_ = f32[64,8]{1,0:T(8,128)} copy(f32[64,8]{0,1:T(8,128)} %param.43) | data formatting | bytes 4096 | tf_op args[17]
  3.4 0.0 copy-done.1
  3.4 0.7 %copy.34.refs_15_ = f32[256,64]{1,0:T(8,128)} copy(f32[256,64]{0,1:T(8,128)S(1)} %copy-done.1) | data formatting | bytes 131072 | tf_op args[15]
  4.2 0.0 copy-done
  4.2 0.8 %copy.36.refs_19_ = f32[512,64]{1,0:T(8,128)} copy(f32[512,64]{0,1:T(8,128)S(1)} %copy-done) | data formatting | bytes 262144 | tf_op args[19]
  5.0 59.3 %step.1 = (f32[1,128]{1,0:T(1,128)}, f32[3,128]{1,0:T(4,128)}, f32[3,128]{1,0:T(4,128)}, f32[3,128]{1,0:T(4,128)}, f32[6,16]{1,0:T(8,128)}, /*index=5*/f32[3,3]{1,0:T(4,128)}, f32[3,3]{1,0:T(4,128)}) custom-call(f32[3,128]{1,0:T(4,128)} %refs_0_.1, f32[3,128]{1,0:T(4,128)} %refs_1_.1, s32[1,128]{1,0:T(1,128)} %bitcast.6, s32[1,192]{1,0:T(1,128)} %bitcast.5, ...), custom_call_target="tpu_custom_call" | custom-call | tf_op jit(solution)/shard_map/step/pallas_call | solution.py:585
  64.3 0.0 copy-start.8
  64.4 0.0 copy-start.7
  64.4 0.6 copy-done.8
  65.0 0.5 copy.44
  65.5 0.0 copy-done.7
  65.5 0.0 copy-start.6
  65.5 0.0 copy-start.5
  65.5 0.6 copy.45
  66.1 0.1 copy-done.6
  66.1 0.0 copy-start.2
  66.1 0.6 copy.46
  66.7 0.0 copy-done.5
  66.7 0.6 copy.47
  67.3 0.0 copy-done.2
  67.3 0.0 copy-start.4
  67.3 0.6 copy.48
  67.9 0.1 copy-done.4
  68.0 0.0 copy-start.3
  68.0 0.6 copy.49
  68.5 0.1 copy-done.3
  68.6 0.6 copy.50
Async XLA Ops:
  0.6 2.8 %copy-start.1 = (f32[256,64]{0,1:T(8,128)S(1)}, f32[256,64]{0,1:T(8,128)}, u32[]{:S(2)}) copy-start(f32[256,64]{0,1:T(8,128)} %param.41) | copy-start | bytes 196612
  0.6 3.5 %copy-start = (f32[512,64]{0,1:T(8,128)S(1)}, f32[512,64]{0,1:T(8,128)}, u32[]{:S(2)}) copy-start(f32[512,64]{0,1:T(8,128)} %param.45) | copy-start | bytes 393220
  64.3 0.6 copy-start.8
  64.4 1.1 %copy-start.7 = (f32[3,128]{1,0:T(4,128)S(1)}, f32[3,128]{1,0:T(4,128)}, u32[]{:S(2)}) copy-start(f32[3,128]{1,0:T(4,128)} %get-tuple-element.29) | copy-start | bytes 4612
  65.5 0.6 copy-start.6
  65.5 1.2 %copy-start.5 = (f32[3,128]{1,0:T(4,128)S(1)}, f32[3,128]{1,0:T(4,128)}, u32[]{:S(2)}) copy-start(f32[3,128]{1,0:T(4,128)} %get-tuple-element.31) | copy-start | bytes 4612
  66.1 1.2 %copy-start.2 = (f32[6,16]{1,0:T(8,128)S(1)}, f32[6,16]{1,0:T(8,128)}, u32[]{:S(2)}) copy-start(f32[6,16]{1,0:T(8,128)} %get-tuple-element.32) | copy-start | bytes 1156
  67.3 0.7 copy-start.4
  68.0 0.7 copy-start.3
where the time goes:
time: 69.7 us; the launch traced here: 69.2 us
  Pallas kernels  59.3 us (85%)
  local copies, waits for them, and re-layouts  9.19 us (13%)
    pallas_call x1, Pallas kernels, body(): pl.pallas_call(functools.partial(kernel, slabs, subs), out_shape=[jax.Sha...  59.3 us
    unnamed x29, local copies, waits for them, and re-layouts  9.19 us

commit v1 on v0

--- a/solution.py
+++ b/solution.py
@@ -1,4 +1,5 @@
 import functools
+import math
 
 import jax
 import jax.numpy as jnp
@@ -53,6 +54,29 @@
     return jnp.concatenate([high, low, high], axis=0)
 
 
+def stack_basis(weights):
+    h, m, l = split3(weights)
+    return jnp.concatenate([h, h, h, m, m, l], axis=0).T.astype(BF16)
+
+
+def stack_out(weights):
+    high = weights.astype(BF16).astype(F32)
+    return jnp.concatenate([high, high, weights - high], axis=0).T.astype(BF16)
+
+
+def sine_cosine(turns):
+    whole = jnp.floor(turns + 0.5)
+    sign = 1.0 - 2.0 * (whole - 2.0 * jnp.floor(0.5 * whole))
+    angle = (turns - whole) * math.pi
+    square = angle * angle
+    sine, cosine = jnp.zeros_like(square), jnp.zeros_like(square)
+    for power in range(6, -1, -1):
+        flip = (-1) ** power
+        sine = sine * square + flip / math.factorial(2 * power + 1)
+        cosine = cosine * square + flip / math.factorial(2 * power)
+    return sine * angle * sign, cosine * sign
+
+
 def mm(left, right):
     return jnp.dot(left, right, preferred_element_type=F32)
 
@@ -66,7 +90,7 @@
 
 
 def logistic(x):
-    return 1.0 / (1.0 + jnp.exp(-x))
+    return 0.5 + 0.5 * jnp.tanh(0.5 * x)
 
 
 def radial_net(start, win, mid0, mid1, out):
@@ -86,8 +110,8 @@
         positions, velocities, species, ghost_species, neighbours, slot_mask, edges, send_slab, send_sub, migrants,
         embedding, energy_shift, masses, one_in, one_mid, one_out, node_one, two_in, two_mid, two_out, node_two,
         readout_linear, readout_hidden, readout_out, box_matrix, box_velocity,
-        energy_out, forces_out, velocities_out, positions_out, arrivals_out, box_out, box_velocity_out,
-        lists, geo, basis, hot, kept1, radial1, radial2, sums, pairs, table, parts, gather_parts,
+        packed_out,
+        lists, geo, element, basis, hot, kept1, slopes1, radial1, radial2, sums, pairs, table, parts, gather_parts,
         packed, gflat, send_a, recv_a, scat, recv_b, push, recv_c, send_d, recv_d, stage1, stage2,
         part1, part2, send_sem, recv_sem, sum_send, sum_recv,
     ) = refs
@@ -127,7 +151,7 @@
 
     def exchange(number, source, target):
         copies = []
-        for block in range(4):
+        for block in (2, 3, 0, 1):
             copy = pltpu.make_async_remote_copy(
                 src_ref=source(block),
                 dst_ref=target(block ^ 1),
@@ -148,7 +172,11 @@
     lists[...] = jnp.zeros_like(lists)
     lists[0:2, 0:GH] = send_slab[...].astype(F32)
     lists[2:4, 0:GH] = send_sub[...].astype(F32)
+    lists[4:5, 0:16] = readout_out[...]
+    lists[5:6, :] = readout_linear[...]
     columns = lists[...].T
+    outer = jnp.broadcast_to(columns[:, 4:5], (C, A))
+    linear = jnp.broadcast_to(columns[:, 5:6], (C, A))
     lanes_f = lax.broadcasted_iota(jnp.int32, (GH, A), 1).astype(F32)
     sent_f = jnp.concatenate(
         [(lanes_f == columns[0:GH, q : q + 1]).astype(F32) for q in range(4)], axis=0
@@ -167,23 +195,26 @@
 
     kinds = lax.broadcasted_iota(jnp.int32, (8, A), 0)
     own_kind = (kinds == species[...]).astype(F32)
-    ghost_kinds = lax.broadcasted_iota(jnp.int32, (8, 4 * GH), 0)
-    ghost_kind = (ghost_kinds == ghost_species[...]).astype(F32)
     pad8 = jnp.zeros((8, A), F32)
-    own_kind16 = jnp.concatenate([own_kind, pad8], axis=0).astype(BF16)
-    ghost_kind16 = jnp.concatenate([ghost_kind, jnp.zeros((8, 4 * GH), F32)], axis=0).astype(BF16)
-
-    orders = (lax.broadcasted_iota(jnp.int32, (8, 1), 0) + 1).astype(F32) * jnp.pi
+    near = neighbours[...]
+    spot, group = near & (A - 1), near >> 7
+
+    def look_up(row):
+        spread = jnp.broadcast_to(row, (K, A))
+        return jnp.take_along_axis(spread, spot, axis=1, mode="promise_in_bounds")
+
+    ghosts = ghost_species[...]
+    tail = jnp.concatenate([ghosts[:, A:], jnp.zeros((1, 2 * A - 4 * GH), jnp.int32)], axis=1)
+    element[...] = jnp.where(
+        group == 0, look_up(species[...]), jnp.where(group == 1, look_up(ghosts[:, 0:A]), look_up(tail))
+    )
+
+    orders = (lax.broadcasted_iota(jnp.int32, (8, 1), 0) + 1).astype(F32)
     scale = jnp.sqrt(2.0 / cutoff).astype(F32)
 
-    one_in_s = jnp.concatenate(
-        [part for part in (lambda h, m, l: (h, h, h, m, m, l))(*split3(one_in[...].T))], axis=0
-    ).T.astype(BF16)
-    two_in_s = jnp.concatenate(
-        [part for part in (lambda h, m, l: (h, h, h, m, m, l))(*split3(two_in[...].T))], axis=0
-    ).T.astype(BF16)
+    one_in_s = stack_basis(one_in[...])
     one_mid0, one_mid1 = stack_left(one_mid[0]), stack_left(one_mid[1])
-    one_out_s = stack_left(one_out[...])
+    one_out_s = stack_out(one_out[...])
 
     lifted = lax.dot_general(
         embedding[...], node_one[0], (((1,), (1,)), ((), ())), precision=HIGHEST, preferred_element_type=F32
@@ -197,10 +228,6 @@
 
     def first_forward(chunk, _):
         here = lanes_of(chunk)
-        row_of = lax.broadcasted_iota(jnp.int32, (EXT, A), 0)
-        for j in range(CH):
-            picked = neighbours[pl.ds(chunk * CH + j, 1), :]
-            hot[chunk, :, j * A : (j + 1) * A] = (row_of == picked).astype(F32).astype(BF16)
         d = geo[4:5, here]
         inverse_d = geo[5:6, here]
         x = d / cutoff
@@ -210,22 +237,29 @@
         x6 = x3 * x3
         envelope = 1.0 - 28.0 * x6 + 48.0 * x6 * x - 21.0 * x6 * x2
         slope = (-168.0 * x5 + 336.0 * x6 - 168.0 * x6 * x) / cutoff
-        angle = orders * x
-        sine, cosine = jnp.sin(angle), jnp.cos(angle)
+        sine, cosine = sine_cosine(orders * x)
         even = scale * inverse_d * envelope
         values = sine * even
-        slopes = cosine * (orders / cutoff) * even + sine * (scale * inverse_d * (slope - envelope * inverse_d))
+        slopes = cosine * (orders * (math.pi / cutoff)) * even + sine * (
+            scale * inverse_d * (slope - envelope * inverse_d)
+        )
         h, m, l = split3(jnp.concatenate([values, slopes], axis=1))
         start = jnp.concatenate([h, m, l, h, m, h], axis=0).astype(BF16)
         basis[chunk] = start
-        radial1[...] = radial_net(start, one_in_s, one_mid0, one_mid1, one_out_s)
-        kind = mm(own_kind16, hot[chunk, 0:A, :]) + mm(ghost_kind16, hot[chunk, A:EXT, :])
-        kind8 = kind[0:8]
+        pre = mm(one_in_s, start[:, 0:W])
+        for layer, after in enumerate((one_mid0, one_mid1, one_out_s)):
+            gate = logistic(pre)
+            active = pre * gate
+            slopes1[chunk, layer * RH : (layer + 1) * RH] = gate + active * (1.0 - gate)
+            pre = mm(after, stack_right(active))
+        radial1[...] = pre
+        kind8 = jnp.concatenate(
+            [(kinds == element[pl.ds(chunk * CH + j, 1), :]).astype(F32) for j in range(CH)], axis=1
+        )
         picked_x = mm(lifted_s, jnp.concatenate([kind8, kind8, kind8, jnp.zeros_like(kind8)], axis=0).astype(BF16))
         total = [jnp.zeros((C, A), F32) for _ in range(4)]
         for j in range(CH):
             cut = slice(j * A, (j + 1) * A)
-            far = slice(W + j * A, W + (j + 1) * A)
             at = pl.ds(pl.multiple_of(chunk * W + j * A, A), A)
             wx = picked_x[:, cut] * geo[3:4, at]
             total[0] += radial1[0:C, cut] * wx
@@ -233,13 +267,21 @@
             for a in range(3):
                 total[a + 1] += geo[a : a + 1, at] * q1
             kept1[chunk, 0:C, cut] = q1
-            kept1[chunk, C : 2 * C, cut] = radial1[0:C, far] * wx
-            kept1[chunk, 2 * C : 3 * C, cut] = radial1[C : 2 * C, far] * wx
+            kept1[chunk, C : 2 * C, cut] = wx
         for a in range(4):
             sums[a] += total[a]
         return 0
 
-    lax.fori_loop(0, NCH, first_forward, 0)
+    def first_slopes(chunk, _):
+        pre = mm(one_in_s, basis[chunk, :, W : 2 * W])
+        for layer, after in enumerate((one_mid0, one_mid1, one_out_s)):
+            pre = mm(after, stack_right(slopes1[chunk, layer * RH : (layer + 1) * RH] * pre))
+        wx = kept1[chunk, C : 2 * C]
+        kept1[chunk, C : 2 * C] = pre[0:C] * wx
+        kept1[chunk, 2 * C : 3 * C] = pre[C : 2 * C] * wx
+        return 0
+
+    lax.fori_loop(0, NCH, first_forward, 0, unroll=True)
 
     s0 = mm(
         jnp.concatenate(list(split3(embedding[...])) + [pad8], axis=0).T.astype(BF16),
@@ -263,14 +305,21 @@
     pl.semaphore_wait(barrier, 4 + many1 - 1 + many2 - 1)
     copies_a = exchange(0, lambda q: send_a.at[rows(q)], lambda q: recv_a.at[rows(q)])
 
+    two_in_s = stack_basis(two_in[...])
     two_mid0, two_mid1 = stack_left(two_mid[0]), stack_left(two_mid[1])
-    two_out_s = stack_left(two_out[...])
+    two_out_s = stack_out(two_out[...])
 
     def second_radial(chunk, _):
+        row_of = lax.broadcasted_iota(jnp.int32, (EXT, A), 0)
+        for j in range(CH):
+            picked = neighbours[pl.ds(chunk * CH + j, 1), :]
+            hot[chunk, :, j * A : (j + 1) * A] = (row_of == picked).astype(F32).astype(BF16)
         radial2[chunk] = radial_net(basis[chunk], two_in_s, two_mid0, two_mid1, two_out_s)
+        own_hot = hot[chunk, 0:A, :]
+        pairs[chunk] = mm(table[...], jnp.concatenate([own_hot, own_hot], axis=0))
         return 0
 
-    lax.fori_loop(0, NCH, second_radial, 0)
+    lax.fori_loop(0, NCH, second_radial, 0, unroll=True)
 
     for copy in copies_a:
         copy.wait_recv()
@@ -282,11 +331,8 @@
     sums2[...] = jnp.zeros_like(sums2)
 
     def second_forward(chunk, _):
-        own_hot = hot[chunk, 0:A, :]
         far_hot = hot[chunk, A:EXT, :]
-        pairs[chunk] = mm(table[...], jnp.concatenate([own_hot, own_hot], axis=0)) + mm(
-            gather_parts[...], jnp.concatenate([far_hot, far_hot], axis=0)
-        )
+        pairs[chunk] += mm(gather_parts[...], jnp.concatenate([far_hot, far_hot], axis=0))
         total = [jnp.zeros((C, A), F32) for _ in range(4)]
         for j in range(CH):
             cut = slice(j * A, (j + 1) * A)
@@ -311,21 +357,20 @@
     b1 = [sums2[1], sums2[2], sums2[3]]
     square2 = b1[0] * b1[0] + b1[1] * b1[1] + b1[2] * b1[2]
     s2 = s1 + mix(node_two[2], b0) + mix(node_two[3], b0 * b0) + mix(node_two[4], square2)
-    pre = mix(readout_hidden[...], s2)
+    inner = jnp.concatenate([readout_hidden[...], jnp.zeros((C - 16, C), F32)], axis=0)
+    pre = mix(inner, s2)
     gate2 = logistic(pre)
     hidden = pre * gate2
-    linear = jnp.broadcast_to(readout_linear[...], (A, C)).T
-    outer = jnp.broadcast_to(readout_out[...], (A, 16)).T
     shift = jnp.zeros((1, A), F32)
     mass = jnp.zeros((1, A), F32)
     for s in range(8):
         shift = jnp.where(species[...] == s, energy_shift[s], shift)
         mass = jnp.where(species[...] == s, masses[s], mass)
-    energy_out[...] = (
+    packed_out[0:1, :] = (
         shift + jnp.sum(linear * s1, axis=0, keepdims=True) + jnp.sum(outer * hidden, axis=0, keepdims=True)
     )
     back_pre = outer * (gate2 + hidden * (1.0 - gate2))
-    back_s2 = mix(readout_hidden[...].T, back_pre)
+    back_s2 = mix(inner.T, back_pre)
     back_b0 = mix(node_two[2].T, back_s2) + 2.0 * b0 * mix(node_two[3].T, back_s2)
     back_square2 = 2.0 * mix(node_two[4].T, back_s2)
     sums2[0] = back_b0
@@ -334,32 +379,44 @@
 
     scat[...] = jnp.zeros_like(scat)
 
-    def second_back(chunk, _):
+    def second_back(side, chunk, _):
         for j in range(CH):
             cut = slice(j * A, (j + 1) * A)
             far = slice(W + j * A, W + (j + 1) * A)
             at = pl.ds(pl.multiple_of(chunk * W + j * A, A), A)
             w = geo[3:4, at]
-            u = [geo[a : a + 1, at] for a in range(3)]
-            wb0 = sums2[0] * w
-            wb1 = [sums2[a + 1] * w for a in range(3)]
-            dot_u = wb1[0] * u[0] + wb1[1] * u[1] + wb1[2] * u[2]
-            back = [radial2[chunk, 0:C, cut] * wb0 + radial2[chunk, C : 2 * C, cut] * dot_u]
-            r3b0 = radial2[chunk, 3 * C : 4 * C, cut] * wb0
+            wu = [w * geo[a : a + 1, at] for a in range(3)]
+            r3 = radial2[chunk, 3 * C : 4 * C, cut]
             r2 = radial2[chunk, 2 * C : 3 * C, cut]
-            for a in range(3):
-                back.append(r3b0 * u[a] + r2 * wb1[a])
-            for a in range(4):
+
+            def vector_part(a):
+                return r3 * (sums2[0] * wu[a]) + r2 * (sums2[a + 1] * w)
+
+            if side == 0:
+                dot_u = sums2[1] * wu[0] + sums2[2] * wu[1] + sums2[3] * wu[2]
+                back = [
+                    radial2[chunk, 0:C, cut] * (sums2[0] * w) + radial2[chunk, C : 2 * C, cut] * dot_u,
+                    vector_part(0),
+                ]
+            else:
+                back = [vector_part(1), vector_part(2)]
+            for a in range(2):
                 h, l = split2(back[a])
                 kept = slice(a * C, (a + 1) * C)
                 packed[kept, cut] = h
                 packed[kept, far] = l
         hot_here = hot[chunk]
-        scat[...] += mm_nt(hot_here, packed[:, 0:W]) + mm_nt(hot_here, packed[:, W : 2 * W])
+        half = slice(side * 2 * C, (side + 1) * 2 * C)
+        scat[:, half] += mm_nt(hot_here, packed[:, 0:W]) + mm_nt(hot_here, packed[:, W : 2 * W])
         return 0
 
-    lax.fori_loop(0, NCH, second_back, 0)
-    copies_b = exchange(1, lambda q: scat.at[pl.ds(A + q * GH, GH)], lambda q: recv_b.at[rows(q)])
+    copies_b = []
+    for side in range(2):
+        lax.fori_loop(0, NCH, functools.partial(second_back, side), 0)
+        half = pl.ds(side * 2 * C, 2 * C)
+        copies_b += exchange(
+            1 + side, lambda q: scat.at[pl.ds(A + q * GH, GH), half], lambda q: recv_b.at[rows(q), half]
+        )
 
     def second_edges(chunk, _):
         for j in range(CH):
@@ -388,6 +445,7 @@
         return 0
 
     lax.fori_loop(0, NCH, second_edges, 0)
+    lax.fori_loop(0, NCH, first_slopes, 0, unroll=True)
 
     for copy in copies_b:
         copy.wait_recv()
@@ -440,7 +498,7 @@
     pushed = push[...]
     pushed = pushed[:, 0:8] + pushed[:, 8:16]
     push[:, 0:8] = pushed
-    copies_c = exchange(2, lambda q: push.at[pl.ds(A + q * GH, GH)], lambda q: recv_c.at[rows(q)])
+    copies_c = exchange(3, lambda q: push.at[pl.ds(A + q * GH, GH)], lambda q: recv_c.at[rows(q)])
 
     own = jnp.zeros((8, A), F32)
     virial = [[jnp.zeros((1, A), F32) for _ in range(3)] for _ in range(3)]
@@ -454,9 +512,9 @@
     come_high, come_low = split2(recv_c[...])
     back_f = (push[0:A] + mm(sent_columns, come_high) + mm(sent_columns, come_low)).T
     forces = own[0:3] - back_f[0:3]
-    forces_out[...] = forces
+    packed_out[8:11, :] = forces
     new_velocities = velocities[...] + time_step * forces / mass
-    velocities_out[...] = new_velocities
+    packed_out[16:19, :] = new_velocities
 
     order = (1, 0, 3, 2)
     movers = jnp.full((1, A), -1, jnp.int32)
@@ -468,7 +526,7 @@
     h, m, l = split3(state)
     sent_state = mm(jnp.concatenate([h, m, l, jnp.zeros_like(h)], axis=0).astype(BF16), chosen)
     send_d[...] = sent_state[0:8] + sent_state[8:16] + sent_state[16:24]
-    copies_d = exchange(3, lambda q: send_d, lambda q: recv_d.at[q])
+    copies_d = exchange(4, lambda q: send_d, lambda q: recv_d.at[q])
 
     mine = jnp.zeros((1, A), F32)
     for a in range(3):
@@ -541,10 +599,10 @@
         box_speed.append(line)
     new_box = [[box[a][b] + time_step * box_speed[a][b] for b in range(3)] for a in range(3)]
     new_inverse = inverse(new_box)
-    for a in range(3):
-        for b in range(3):
-            box_out[a : a + 1, b : b + 1] = new_box[a][b][:, 0:1]
-            box_velocity_out[a : a + 1, b : b + 1] = box_speed[a][b][:, 0:1]
+    for group_at, matrix in ((40, new_box), (48, box_speed)):
+        for a in range(3):
+            line = jnp.where(lane == 0, matrix[a][0], jnp.where(lane == 1, matrix[a][1], matrix[a][2]))
+            packed_out[group_at + a : group_at + a + 1, :] = line
 
     def drift(moving):
         return [
@@ -554,7 +612,7 @@
 
     moved = drift(new_velocities)
     for a in range(3):
-        positions_out[a : a + 1, :] = positions[a : a + 1, :] + time_step * moved[a]
+        packed_out[24 + a : 25 + a, :] = positions[a : a + 1, :] + time_step * moved[a]
     for copy in copies_d:
         copy.wait_recv()
     come = jnp.where(
@@ -562,12 +620,17 @@
     )
     moved = drift(come[3:6])
     for a in range(3):
-        arrivals_out[a : a + 1, :] = (come[a : a + 1] + time_step * moved[a])[:, 0:16]
-    arrivals_out[3:6, :] = come[3:6, 0:16]
+        packed_out[32 + a : 33 + a, :] = come[a : a + 1] + time_step * moved[a]
+    packed_out[35:38, :] = come[3:6]
 
     for copies in (copies_a, copies_b, copies_c, copies_d):
         for copy in copies:
             copy.wait_send()
+
+
+def unpack(held, *outs):
+    for i, out in enumerate(outs):
+        out[...] = held[8 * i : 8 * i + out.shape[0], 0 : out.shape[1]]
 
 
 def solution(mesh):
@@ -581,26 +644,30 @@
         arrays = list(arrays)
         for position in (2, 3, 21, 23):
             arrays[position] = arrays[position].reshape(1, -1)
+        for position in (13, 15, 17, 19):
+            arrays[position] = arrays[position].T
         shapes = [(1, A), (3, A), (3, A), (3, A), (6, 16), (3, 3), (3, 3)]
-        outs = pl.pallas_call(
+        held = pl.pallas_call(
             functools.partial(kernel, slabs, subs),
-            out_shape=[jax.ShapeDtypeStruct(shape, F32) for shape in shapes],
+            out_shape=jax.ShapeDtypeStruct((8 * len(shapes), A), F32),
             in_specs=[smem if i in in_smem else vmem for i in range(26)],
-            out_specs=[vmem] * 7,
+            out_specs=vmem,
             scratch_shapes=[
                 pltpu.VMEM((8, 128), F32),
                 pltpu.VMEM((8, E), F32),
+                pltpu.VMEM((K, A), jnp.int32),
                 pltpu.VMEM((NCH, 48, 2 * W), BF16),
                 pltpu.VMEM((NCH, EXT, W), BF16),
                 pltpu.VMEM((NCH, 3 * C, W), F32),
-                pltpu.VMEM((2 * C, 2 * W), F32),
+                pltpu.VMEM((NCH, 3 * RH, W), F32),
+                pltpu.VMEM((2 * C, W), F32),
                 pltpu.VMEM((NCH, 4 * C, 2 * W), F32),
                 pltpu.VMEM((4, C, A), F32),
                 pltpu.VMEM((NCH, 4 * C, W), F32),
                 pltpu.VMEM((4 * C, 2 * A), BF16),
                 pltpu.VMEM((4, C, A), F32),
                 pltpu.VMEM((4 * C, 8 * GH), BF16),
-                pltpu.VMEM((4 * C, 2 * W), BF16),
+                pltpu.VMEM((2 * C, 2 * W), BF16),
                 pltpu.VMEM((8, E), F32),
                 pltpu.VMEM((4 * GH, 4 * C), F32),
                 pltpu.VMEM((4 * GH, 4 * C), F32),
@@ -614,8 +681,8 @@
                 pltpu.VMEM((many2, 1, A), F32),
                 pltpu.VMEM((1, 1, A), F32),
                 pltpu.VMEM((1, 1, A), F32),
-                pltpu.SemaphoreType.DMA((4, 4)),
-                pltpu.SemaphoreType.DMA((4, 4)),
+                pltpu.SemaphoreType.DMA((5, 4)),
+                pltpu.SemaphoreType.DMA((5, 4)),
                 pltpu.SemaphoreType.DMA((2,)),
                 pltpu.SemaphoreType.DMA((2,)),
             ],
@@ -624,6 +691,13 @@
             ),
             name="step",
         )(*arrays)
+        outs = pl.pallas_call(
+            unpack,
+            out_shape=[jax.ShapeDtypeStruct(shape, F32) for shape in shapes],
+            in_specs=[vmem],
+            out_specs=[vmem] * 7,
+            name="unpack",
+        )(held)
         return (outs[0].reshape(A),) + tuple(outs[1:])
 
     tail = P(None, ("slab", "sub"))

time: 69.7 us -> 57.1 us (0.82)
  local copies, waits for them, and re-layouts: 9.19 us -> 0 us
  Pallas kernels: 59.3 us -> 56.3 us
    unnamed x29 -> x0, local copies, waits for them, and re-layouts: 9.19 us -> none
    pallas_call x1 -> x2, Pallas kernels: 59.3 us -> 56.3 us  [the longest x1 54.9 us: body(): pl.pallas_call(functools.partial(kernel, slabs, subs), out_shape=jax.Shap...]
where the time goes in v1:
time: 57.1 us; the launch traced here: 56.9 us
  Pallas kernels  56.3 us (99%)
  between operations  0.65 us (1%)
    pallas_call x1, Pallas kernels, body(): pl.pallas_call(functools.partial(kernel, slabs, subs), out_shape=jax.Shap...  54.9 us
    pallas_call x1, Pallas kernels, body(): pl.pallas_call(unpack, out_shape=[jax.ShapeDtypeStruct(shape, F32) for sh...  1.37 us

profile of v1, /device:TPU:8, one launch (start us, length us, event | category | flops | bytes accessed | tf_op | source)
XLA Modules:
  0.0 56.9 jit_solution(3777962445443974169)
XLA Ops:
  0.6 54.9 %step.1.held = f32[56,128]{1,0:T(8,128)} custom-call(f32[3,128]{1,0:T(4,128)} %refs_0_.1, f32[3,128]{1,0:T(4,128)} %refs_1_.1, s32[1,128]{1,0:T(1,128)} %bitcast.14, s32[1,192]{1,0:T(1,128)} %bitcast.13, s32[20,128]{1,0:T(8,128)} %refs_4_.1, s32[20,128]{1,0:T(8,128)} %refs_5_.1, f32[3,20,128]{2,1,0:T(8,128)} %refs_6_.1, s32[2,48]{1,0:T(2,128)} %refs_7_.1, ...), custom_call_target="tpu_custom_call" | custom-call | tf_op jit(solution)/shard_map/step/pallas_call | solution.py:650
  55.6 1.4 %unpack.1 = (f32[1,128]{1,0:T(1,128)}, f32[3,128]{1,0:T(4,128)}, f32[3,128]{1,0:T(4,128)}, f32[3,128]{1,0:T(4,128)}, f32[6,16]{1,0:T(8,128)}, /*index=5*/f32[3,3]{1,0:T(4,128)}, f32[3,3]{1,0:T(4,128)}) custom-call(f32[56,128]{1,0:T(8,128)} %step.1.held), custom_call_target="tpu_custom_call" | custom-call | tf_op jit(solution)/shard_map/unpack/pallas_call | solution.py:694

commit v2 on v1

--- a/solution.py
+++ b/solution.py
@@ -320,6 +320,7 @@
         return 0
 
     lax.fori_loop(0, NCH, second_radial, 0, unroll=True)
+    lax.fori_loop(0, NCH, first_slopes, 0, unroll=True)
 
     for copy in copies_a:
         copy.wait_recv()
@@ -377,13 +378,12 @@
     for a in range(3):
         sums2[a + 1] = b1[a] * back_square2
 
-    scat[...] = jnp.zeros_like(scat)
-
-    def second_back(side, chunk, _):
+
+    def second_back(side, chunk):
         for j in range(CH):
             cut = slice(j * A, (j + 1) * A)
             far = slice(W + j * A, W + (j + 1) * A)
-            at = pl.ds(pl.multiple_of(chunk * W + j * A, A), A)
+            at = pl.ds(chunk * W + j * A, A)
             w = geo[3:4, at]
             wu = [w * geo[a : a + 1, at] for a in range(3)]
             r3 = radial2[chunk, 3 * C : 4 * C, cut]
@@ -403,17 +403,17 @@
             for a in range(2):
                 h, l = split2(back[a])
                 kept = slice(a * C, (a + 1) * C)
-                packed[kept, cut] = h
-                packed[kept, far] = l
-        hot_here = hot[chunk]
-        half = slice(side * 2 * C, (side + 1) * 2 * C)
-        scat[:, half] += mm_nt(hot_here, packed[:, 0:W]) + mm_nt(hot_here, packed[:, W : 2 * W])
-        return 0
+                packed[side, chunk, kept, cut] = h
+                packed[side, chunk, kept, far] = l
+        return mm_nt(hot[chunk], packed[side, chunk, :, 0:W]) + mm_nt(hot[chunk], packed[side, chunk, :, W : 2 * W])
 
     copies_b = []
     for side in range(2):
-        lax.fori_loop(0, NCH, functools.partial(second_back, side), 0)
         half = pl.ds(side * 2 * C, 2 * C)
+        gathered = second_back(side, 0)
+        for chunk in range(1, NCH):
+            gathered += second_back(side, chunk)
+        scat[:, half] = gathered
         copies_b += exchange(
             1 + side, lambda q: scat.at[pl.ds(A + q * GH, GH), half], lambda q: recv_b.at[rows(q), half]
         )
@@ -445,7 +445,6 @@
         return 0
 
     lax.fori_loop(0, NCH, second_edges, 0)
-    lax.fori_loop(0, NCH, first_slopes, 0, unroll=True)
 
     for copy in copies_b:
         copy.wait_recv()
@@ -494,7 +493,7 @@
         push[...] += mm_nt(hot[chunk], both)
         return 0
 
-    lax.fori_loop(0, NCH, first_edges, 0)
+    lax.fori_loop(0, NCH, first_edges, 0, unroll=True)
     pushed = push[...]
     pushed = pushed[:, 0:8] + pushed[:, 8:16]
     push[:, 0:8] = pushed
@@ -667,7 +666,7 @@
                 pltpu.VMEM((4 * C, 2 * A), BF16),
                 pltpu.VMEM((4, C, A), F32),
                 pltpu.VMEM((4 * C, 8 * GH), BF16),
-                pltpu.VMEM((2 * C, 2 * W), BF16),
+                pltpu.VMEM((2, NCH, 2 * C, 2 * W), BF16),
                 pltpu.VMEM((8, E), F32),
                 pltpu.VMEM((4 * GH, 4 * C), F32),
                 pltpu.VMEM((4 * GH, 4 * C), F32),

time: 57.1 us -> 55.8 us (0.977)
  Pallas kernels: 56.3 us -> 55 us
    pallas_call x1, Pallas kernels: 54.9 us -> 53.7 us  [body(): pl.pallas_call(functools.partial(kernel, slabs, subs), out_shape=jax.Shap...]
where the time goes in v2:
time: 55.8 us; the launch traced here: 55.7 us
  Pallas kernels  55 us (99%)
  between operations  0.65 us (1%)
    pallas_call x1, Pallas kernels, body(): pl.pallas_call(functools.partial(kernel, slabs, subs), out_shape=jax.Shap...  53.7 us
    pallas_call x1, Pallas kernels, body(): pl.pallas_call(unpack, out_shape=[jax.ShapeDtypeStruct(shape, F32) for sh...  1.37 us

profile of v2, /device:TPU:8, one launch (start us, length us, event | category | flops | bytes accessed | tf_op | source)
XLA Modules:
  0.0 55.7 jit_solution(1823579209117568265)
XLA Ops:
  0.6 53.7 %step.1.held = f32[56,128]{1,0:T(8,128)} custom-call(f32[3,128]{1,0:T(4,128)} %refs_0_.1, f32[3,128]{1,0:T(4,128)} %refs_1_.1, s32[1,128]{1,0:T(1,128)} %bitcast.14, s32[1,192]{1,0:T(1,128)} %bitcast.13, s32[20,128]{1,0:T(8,128)} %refs_4_.1, s32[20,128]{1,0:T(8,128)} %refs_5_.1, f32[3,20,128]{2,1,0:T(8,128)} %refs_6_.1, s32[2,48]{1,0:T(2,128)} %refs_7_.1, ...), custom_call_target="tpu_custom_call" | custom-call | tf_op jit(solution)/shard_map/step/pallas_call | solution.py:649
  54.3 1.4 %unpack.1 = (f32[1,128]{1,0:T(1,128)}, f32[3,128]{1,0:T(4,128)}, f32[3,128]{1,0:T(4,128)}, f32[3,128]{1,0:T(4,128)}, f32[6,16]{1,0:T(8,128)}, /*index=5*/f32[3,3]{1,0:T(4,128)}, f32[3,3]{1,0:T(4,128)}) custom-call(f32[56,128]{1,0:T(8,128)} %step.1.held), custom_call_target="tpu_custom_call" | custom-call | tf_op jit(solution)/shard_map/unpack/pallas_call | solution.py:693

commit v3 on v2

--- a/solution.py
+++ b/solution.py
@@ -337,7 +337,7 @@
         total = [jnp.zeros((C, A), F32) for _ in range(4)]
         for j in range(CH):
             cut = slice(j * A, (j + 1) * A)
-            at = pl.ds(pl.multiple_of(chunk * W + j * A, A), A)
+            at = pl.ds(chunk * W + j * A, A)
             w = geo[3:4, at]
             u = [geo[a : a + 1, at] for a in range(3)]
             wx = pairs[chunk, 0:C, cut] * w
@@ -352,7 +352,12 @@
             sums2[a] += total[a]
         return 0
 
-    lax.fori_loop(0, NCH, second_forward, 0)
+    def all_second_forward(_, carry):
+        for chunk in range(NCH):
+            second_forward(chunk, 0)
+        return carry
+
+    lax.fori_loop(0, 1 + slab // slabs, all_second_forward, 0)
 
     b0 = sums2[0]
     b1 = [sums2[1], sums2[2], sums2[3]]

time: 55.8 us -> 55.1 us (0.987)
  Pallas kernels: 55 us -> 54.3 us
    pallas_call x1, Pallas kernels: 53.7 us -> 52.9 us  [body(): pl.pallas_call(functools.partial(kernel, slabs, subs), out_shape=jax.Shap...]
where the time goes in v3:
time: 55.1 us; the launch traced here: 55 us
  Pallas kernels  54.3 us (99%)
  between operations  0.65 us (1%)
    pallas_call x1, Pallas kernels, body(): pl.pallas_call(functools.partial(kernel, slabs, subs), out_shape=jax.Shap...  52.9 us
    pallas_call x1, Pallas kernels, body(): pl.pallas_call(unpack, out_shape=[jax.ShapeDtypeStruct(shape, F32) for sh...  1.37 us

profile of v3, /device:TPU:8, one launch (start us, length us, event | category | flops | bytes accessed | tf_op | source)
XLA Modules:
  0.0 55.0 jit_solution(5360498129786455072)
XLA Ops:
  0.6 52.9 %step.1.held = f32[56,128]{1,0:T(8,128)} custom-call(f32[3,128]{1,0:T(4,128)} %refs_0_.1, f32[3,128]{1,0:T(4,128)} %refs_1_.1, s32[1,128]{1,0:T(1,128)} %bitcast.14, s32[1,192]{1,0:T(1,128)} %bitcast.13, s32[20,128]{1,0:T(8,128)} %refs_4_.1, s32[20,128]{1,0:T(8,128)} %refs_5_.1, f32[3,20,128]{2,1,0:T(8,128)} %refs_6_.1, s32[2,48]{1,0:T(2,128)} %refs_7_.1, ...), custom_call_target="tpu_custom_call" | custom-call | tf_op jit(solution)/shard_map/step/pallas_call | solution.py:654
  53.6 1.4 %unpack.1 = (f32[1,128]{1,0:T(1,128)}, f32[3,128]{1,0:T(4,128)}, f32[3,128]{1,0:T(4,128)}, f32[3,128]{1,0:T(4,128)}, f32[6,16]{1,0:T(8,128)}, /*index=5*/f32[3,3]{1,0:T(4,128)}, f32[3,3]{1,0:T(4,128)}) custom-call(f32[56,128]{1,0:T(8,128)} %step.1.held), custom_call_target="tpu_custom_call" | custom-call | tf_op jit(solution)/shard_map/unpack/pallas_call | solution.py:698

commit v4 on v3

--- a/solution.py
+++ b/solution.py
@@ -538,12 +538,11 @@
             term = new_velocities[a : a + 1] * mass * new_velocities[b : b + 1] - virial[a][b]
             mine = jnp.where(lane == 3 * a + b, jnp.sum(term, axis=1, keepdims=True), mine)
 
-    def all_sum(number, value, part, stage, many, me, peer):
+    def all_sum(number, value, part, stage, many, me, peer, ring):
         part[...] = value.reshape(1, 1, A)
         stage[pl.ds(me, 1)] = value.reshape(1, 1, A)
 
-        @pl.loop(1, many)
-        def _(step):
+        for step in sorted(range(1, many), key=lambda step: -min(step % ring, ring - step % ring)):
             pltpu.make_async_remote_copy(
                 src_ref=part,
                 dst_ref=stage.at[pl.ds(me, 1)],
@@ -558,8 +557,8 @@
         pltpu.make_async_copy(whole, whole, sum_send.at[number]).wait()
         return jnp.sum(stage[...], axis=0)
 
-    near = all_sum(0, mine, part1, stage1, many1, mine1, first_peer)
-    stress_row = all_sum(1, near, part2, stage2, many2, high, second_peer)
+    near = all_sum(0, mine, part1, stage1, many1, mine1, first_peer, subs)
+    stress_row = all_sum(1, near, part2, stage2, many2, high, second_peer, many2)
 
     def entry(ref, a, b):
         return jnp.full((1, A), ref[a, b], F32)

time: 55.1 us -> 55 us (level)
  no operation moved by 1% of the time
where the time goes in v4:
time: 55 us; the launch traced here: 54.8 us
  Pallas kernels  54.1 us (98%)
  between operations  0.65 us (1%)
    pallas_call x1, Pallas kernels, body(): pl.pallas_call(functools.partial(kernel, slabs, subs), out_shape=jax.Shap...  52.7 us
    pallas_call x1, Pallas kernels, body(): pl.pallas_call(unpack, out_shape=[jax.ShapeDtypeStruct(shape, F32) for sh...  1.37 us

profile of v4, /device:TPU:8, one launch (start us, length us, event | category | flops | bytes accessed | tf_op | source)
XLA Modules:
  0.0 54.8 jit_solution(15763662667243799777)
XLA Ops:
  0.6 52.7 %step.1.held = f32[56,128]{1,0:T(8,128)} custom-call(f32[3,128]{1,0:T(4,128)} %refs_0_.1, f32[3,128]{1,0:T(4,128)} %refs_1_.1, s32[1,128]{1,0:T(1,128)} %bitcast.14, s32[1,192]{1,0:T(1,128)} %bitcast.13, s32[20,128]{1,0:T(8,128)} %refs_4_.1, s32[20,128]{1,0:T(8,128)} %refs_5_.1, f32[3,20,128]{2,1,0:T(8,128)} %refs_6_.1, s32[2,48]{1,0:T(2,128)} %refs_7_.1, ...), custom_call_target="tpu_custom_call" | custom-call | tf_op jit(solution)/shard_map/step/pallas_call | solution.py:653
  53.4 1.4 %unpack.1 = (f32[1,128]{1,0:T(1,128)}, f32[3,128]{1,0:T(4,128)}, f32[3,128]{1,0:T(4,128)}, f32[3,128]{1,0:T(4,128)}, f32[6,16]{1,0:T(8,128)}, /*index=5*/f32[3,3]{1,0:T(4,128)}, f32[3,3]{1,0:T(4,128)}) custom-call(f32[56,128]{1,0:T(8,128)} %step.1.held), custom_call_target="tpu_custom_call" | custom-call | tf_op jit(solution)/shard_map/unpack/pallas_call | solution.py:697
